TPU v7x, 256 devices: a whole 4x4x8 slice. The times are simulated.
256 devices in a mesh: mp: 8 (over z_lo, core), seq: 32 (over x, z_hi, y).
Axes of the slice: x: 4, y: 4, z: 8 (z_hi: 2, z_lo: 4; z = z_hi * 4 + z_lo), core: 2. Of those that a mesh axis runs over, the one named last changes fastest.
Arguments:
- noise_gen: bfloat16 [8, 1024, 64], P('mp', 'seq'), may hold values from -6 to 6
- noise_add: bfloat16 [8, 1024, 64], P('mp', 'seq'), may hold values from -6 to 6
- steps_t: int32 [4], replicated, may hold values from 20 to 979
- gen_in: bfloat16 [64, 5120], replicated, may hold values from -0.75 to 0.75
- gen_out: bfloat16 [5120, 64], replicated, may hold values from -0.078125 to 0.078125
- real_in: bfloat16 [64, 5120], replicated, may hold values from -0.75 to 0.75
- real_qkv: bfloat16 [5120, 3, 32, 128], P('mp', None, 'seq'), may hold values from -2.5 to 2.5
- real_proj: bfloat16 [32, 128, 5120], P('seq', None, 'mp'), may hold values from -0.09375 to 0.09375
- real_head: bfloat16 [5120, 64], replicated, may hold values from -0.078125 to 0.078125
- fake_in: bfloat16 [64, 5120], replicated, may hold values from -0.75 to 0.75
- fake_qkv: bfloat16 [5120, 3, 32, 128], P('mp', None, 'seq'), may hold values from -2.5 to 2.5
- fake_proj: bfloat16 [32, 128, 5120], P('seq', None, 'mp'), may hold values from -0.09375 to 0.09375
- fake_head: bfloat16 [5120, 64], replicated, may hold values from -0.078125 to 0.078125
Outputs:
- dmd_grad: float32 [8, 1024, 64], P('mp', 'seq')
- grad_in: float32 [64, 5120], P(None, 'seq')
- grad_out: float32 [5120, 64], P('seq')
All inputs are finite; a program needn't handle non-finite values.
Results may differ from a plain program's by a relative error of at most 0.01.
Values may be sent and summed in bfloat16 or wider, within the bound.
A program may use at most 128 MiB of HBM per device.

v0:
```python
import math

import jax
import jax.numpy as jnp
from jax import lax
from jax.sharding import PartitionSpec as P


def from_partner(value, axis, stride):
    mask = 2**stride
    pairs = [(source, source ^ mask) for source in range(lax.axis_size(axis))]
    return lax.ppermute(value, axis, pairs)


def attend(packed):
    queries = packed[:, 0]
    keys_all = packed[:, 1]
    values_all = packed[:, 2]
    length_all = queries.shape[0]
    heads_here = queries.shape[1]
    head_size = queries.shape[2]
    block_rows = min(512, length_all)
    inv_root = 1.0 / math.sqrt(head_size)

    def one_block(query_rows):
        scores = (
            jnp.einsum("qnh,knh->nqk", query_rows, keys_all, preferred_element_type=jnp.float32)
            * inv_root
        )
        row_max = jnp.max(scores, axis=-1, keepdims=True)
        weights = jnp.exp(scores - row_max)
        probs = (weights / jnp.sum(weights, axis=-1, keepdims=True)).astype(jnp.bfloat16)
        return jnp.einsum(
            "nqk,knh->qnh", probs, values_all, preferred_element_type=jnp.float32
        ).astype(jnp.bfloat16)

    query_blocks = queries.reshape(length_all // block_rows, block_rows, heads_here, head_size)
    return lax.map(one_block, query_blocks).reshape(length_all, heads_here, head_size)


def score_model(tokens, embed, table, proj, head):
    heads_here = table.shape[2]
    head_size = table.shape[3]
    flat_table = table.reshape(table.shape[0], 3 * heads_here * head_size)
    own_stream = jnp.dot(tokens, embed, preferred_element_type=jnp.float32).astype(jnp.bfloat16)
    flat_packed = jnp.dot(
        lax.all_gather(own_stream, "seq", axis=0, tiled=True),
        flat_table,
        preferred_element_type=jnp.float32,
    ).astype(jnp.bfloat16)
    packed = flat_packed.reshape(flat_packed.shape[0], 3, heads_here, head_size)
    attended = attend(packed)
    flat_attended = attended.reshape(attended.shape[0], heads_here * head_size)
    mixed = jnp.einsum("nhd,dp->nhp", proj, head, preferred_element_type=jnp.float32).reshape(
        heads_here * head_size, head.shape[1]
    )
    branch = lax.psum_scatter(
        jnp.dot(flat_attended.astype(jnp.float32), mixed, precision=lax.Precision.HIGHEST),
        "seq",
        scatter_dimension=0,
        tiled=True,
    )
    return branch + jnp.dot(own_stream, head, preferred_element_type=jnp.float32)


def body(
    noise_gen,
    noise_add,
    steps_t,
    gen_in,
    gen_out,
    real_in,
    real_qkv,
    real_proj,
    real_head,
    fake_in,
    fake_qkv,
    fake_proj,
    fake_head,
):
    role_index = lax.axis_index("mp") % 2
    clip_index = lax.axis_index("mp") // 2
    noise_level = (
        lax.dynamic_index_in_dim(steps_t, clip_index, 0, False).astype(jnp.float32) / 1000.0
    )
    own_noise = noise_gen[0]
    half_rows = own_noise.shape[0]
    pre_act = jnp.dot(own_noise, gen_in, preferred_element_type=jnp.float32)
    hidden = jax.nn.silu(pre_act).astype(jnp.bfloat16)
    clean_guess = own_noise.astype(jnp.float32) + jnp.dot(
        hidden, gen_out, preferred_element_type=jnp.float32
    )
    noised = (
        (1.0 - noise_level) * clean_guess + noise_level * noise_add[0].astype(jnp.float32)
    ).astype(jnp.bfloat16)
    partner = from_partner(noised, "mp", 0)
    is_real = role_index == 0
    tokens = jnp.concatenate(
        [jnp.where(is_real, noised, partner), jnp.where(is_real, partner, noised)], axis=0
    )
    real_table, fake_table, real_wide, fake_wide = (
        lax.all_gather(real_qkv, "mp", axis=0, tiled=True),
        lax.all_gather(fake_qkv, "mp", axis=0, tiled=True),
        lax.all_gather(real_proj, "mp", axis=2, tiled=True),
        lax.all_gather(fake_proj, "mp", axis=2, tiled=True),
    )
    table = jnp.where(is_real, real_table, fake_table)
    proj = jnp.where(is_real, real_wide, fake_wide)
    embed = jnp.where(is_real, real_in, fake_in)
    head = jnp.where(is_real, real_head, fake_head)
    velocity = score_model(tokens, embed, table, proj, head)
    mine_half = lax.dynamic_slice_in_dim(velocity, role_index * half_rows, half_rows, 0)
    partner_half = lax.dynamic_slice_in_dim(velocity, (1 - role_index) * half_rows, half_rows, 0)
    received = from_partner(partner_half, "mp", 0)
    velocity_real = jnp.where(is_real, mine_half, received)
    velocity_fake = jnp.where(is_real, received, mine_half)
    dmd_grad = noise_level * (velocity_real - velocity_fake)
    rows_total = lax.axis_size("mp") // 2 * tokens.shape[0] * lax.axis_size("seq")
    loss_scale = 1.0 / math.sqrt(rows_total)
    scaled = (dmd_grad * loss_scale).astype(jnp.bfloat16)
    grad_out = jnp.einsum("td,tp->dp", hidden, scaled, preferred_element_type=jnp.float32)
    back_hidden = jnp.einsum("tp,dp->td", scaled, gen_out, preferred_element_type=jnp.float32)
    sigmoid_pre = jax.nn.sigmoid(pre_act)
    pre_grad = (back_hidden * sigmoid_pre * (1.0 + pre_act * (1.0 - sigmoid_pre))).astype(
        jnp.bfloat16
    )
    grad_in = jnp.einsum("tp,td->pd", own_noise, pre_grad, preferred_element_type=jnp.float32)
    grad_in, grad_out = (
        lax.psum_scatter(grad_in, "seq", scatter_dimension=1, tiled=True),
        lax.psum_scatter(grad_out, "seq", scatter_dimension=0, tiled=True),
    )
    grad_in, grad_out = lax.psum((grad_in, grad_out), "mp")
    return (dmd_grad[None], grad_in, grad_out)


def solution(mesh):
    return jax.shard_map(
        body,
        mesh=mesh,
        in_specs=(
            P("mp", "seq", None),
            P("mp", "seq", None),
            P(),
            P(),
            P(),
            P(),
            P("mp", None, "seq", None),
            P("seq", None, "mp"),
            P(),
            P(),
            P("mp", None, "seq", None),
            P("seq", None, "mp"),
            P(),
        ),
        out_specs=(P("mp", "seq", None), P(None, "seq"), P("seq", None)),
        check_vma=False,
    )
```

profile of v0, /device:TPU:1, one launch (start us, length us, event | category | flops | bytes accessed | tf_op | source)
XLA Modules:
  0.0 1270.0 jit_solution(2893376147759586602)
XLA Ops:
  7.2 0.0 all-gather.12.cloned.1.call-start
  7.2 0.7 all-gather.12.cloned.1.call-update
  8.0 0.0 all-gather.14.cloned.1.call-start
  8.0 0.7 all-gather.14.cloned.1.call-update
  8.7 0.0 all-gather.10.cloned.1.call-start
  8.8 2.0 copy.26
  10.8 0.0 all-gather.10.cloned.1.call-update
  10.8 0.0 all-gather.8.cloned.1.call-start
  10.8 2.0 copy.25
  12.9 0.0 all-gather.8.cloned.1.call-update
  12.9 0.0 all-gather.6.cloned.1.call-start
  13.0 1.3 dynamic_slice.14
  14.9 1.3 fusion.31
  16.3 0.3 fusion.20
  16.6 3.3 collective-permute-start
  19.9 0.8 collective-permute-done
  20.8 1.2 convolution_convert_fusion
  22.0 0.0 all-gather.6.cloned.1.call-update
  22.0 0.0 reduce-scatter.8.cloned.1.call-start
  22.0 26.5 %all-gather.12.cloned.1.call-done = bf16[1,128,5120]{2,1,0:T(8,128)(2,1)} async-done(((bf16[1,128,640]{2,1,0:T(8,128)(2,1)}), bf16[1,128,5120]{2,1,0:T(8,128)(2,1)}) %all-gather.12.cloned.1.call-update) | async-done | bytes 1310736 | tf_op jit(solution)/shard_map/all_gather | solution.py:104
  48.6 38.6 %all-gather.14.cloned.1.call-done = bf16[1,128,5120]{2,1,0:T(8,128)(2,1)} async-done(((bf16[1,128,640]{2,1,0:T(8,128)(2,1)}), bf16[1,128,5120]{2,1,0:T(8,128)(2,1)}) %all-gather.14.cloned.1.call-update) | async-done | bytes 1310736 | tf_op jit(solution)/shard_map/all_gather | solution.py:105
  87.2 2.6 fusion.14
  89.8 51.0 %all-gather.10.cloned.1.call-done = bf16[5120,3,1,128]{0,3,1,2:T(8,128)(2,1)} async-done(((bf16[640,3,1,128]{0,3,1,2:T(8,128)(2,1)}), bf16[5120,3,1,128]{0,3,1,2:T(8,128)(2,1)}) %all-gather.10.cloned.1.call-update) | async-done | bytes 3932176 | tf_op jit(solution)/shard_map/all_gather | solution.py:103
  140.8 52.5 %all-gather.8.cloned.1.call-done = bf16[5120,3,1,128]{0,3,1,2:T(8,128)(2,1)} async-done(((bf16[640,3,1,128]{0,3,1,2:T(8,128)(2,1)}), bf16[5120,3,1,128]{0,3,1,2:T(8,128)(2,1)}) %all-gather.8.cloned.1.call-update) | async-done | bytes 3932176 | tf_op jit(solution)/shard_map/all_gather | solution.py:102
  193.4 4.4 broadcast_select_fusion
  197.8 292.0 %all-gather.6.cloned.1.call-done = bf16[2048,5120]{1,0:T(8,128)(2,1)} async-done(((bf16[64,5120]{1,0:T(8,128)(2,1)}), bf16[2048,5120]{1,0:T(8,128)(2,1)}) %all-gather.6.cloned.1.call-update) | async-done | bytes 20971536 | tf_op jit(solution)/shard_map/all_gather | solution.py:47
  489.7 13.6 %convolution_convert_fusion.1 = bf16[2048,384]{0,1:T(8,128)(2,1)S(1)} fusion(bf16[2048,5120]{1,0:T(8,128)(2,1)} %all-gather.6.cloned.1.call-done, bf16[5120,384]{0,1:T(8,128)(2,1)} %bitcast.67), kind=kOutput, calls=%fused_computation.21 | convolution fusion | flops 8053850112 | bytes 26476544 | tf_op jit(solution)/shard_map/dot_general | solution.py:46
  503.4 0.1 fusion.39
  503.5 0.3 copy.35
  503.7 0.3 copy.36
  504.0 0.3 copy.37
  504.3 13.1 %while.10 = (s32[]{:T(128)}, bf16[4,512,1,128]{3,1,2,0:T(8,128)(2,1)}, bf16[4,512,1,128]{3,1,2,0:T(8,128)(2,1)S(1)}, bf16[2048,1,128]{2,0,1:T(8,128)(2,1)S(1)}, bf16[2048,1,128]{2,0,1:T(8,128)(2,1)S(1)}, /*index=5*/s32[]{:T(128)}) while((s32[]{:T(128)}, bf16[4,512,1,128]{3,1,2,0:T(8,128)(2,1)}, bf16[4,512,1,128]{3,1,2,0:T(8,128)(2,1)S(1)}, ...), condition=%wide.region_3.4_spmd, body=%wide.region_0.3_spmd.sunk | while | flops 546372608 | bytes 13904457 | solution.py:38
  504.3 0.8 multiply_reduce_fusion.2
  505.1 0.8 fusion.53
  505.9 1.6 fusion.54
  507.6 0.8 multiply_reduce_fusion.2
  508.4 0.8 fusion.53
  509.2 1.6 fusion.54
  510.9 0.8 multiply_reduce_fusion.2
  511.6 0.8 fusion.53
  512.5 1.7 fusion.54
  514.1 0.8 multiply_reduce_fusion.2
  514.9 0.8 fusion.53
  515.7 1.7 fusion.54
  517.4 2.6 fusion.40
  520.0 0.0 reduce-scatter.8.cloned.1.call-update
  520.0 0.0 reduce-scatter.10.cloned.1.call-start
  520.1 196.0 %reduce-scatter.8.cloned.1.call-done = f32[64,64]{1,0:T(8,128)} async-done(((f32[2048,64]{1,0:T(8,128)}), f32[64,64]{1,0:T(8,128)}) %reduce-scatter.8.cloned.1.call-update) | async-done | bytes 16400 | tf_op jit(solution)/shard_map/reduce_scatter | solution.py:57
  716.1 1.5 convolution_add_fusion
  717.6 26.3 %collective-permute-start.1 = (f32[32,64]{1,0:T(8,128)S(1)}, f32[32,64]{1,0:T(8,128)S(1)}, u32[]{:S(2)}, u32[]{:S(2)}) collective-permute-start(f32[32,64]{1,0:T(8,128)S(1)} %constant_dynamic-slice_fusion), channel_id=1, source_target_pairs={{0,32},{32,0},{64,96},{96,64},{128,160},{160,128},{192,224},{224,1... | collective-permute-start | bytes 24584 | tf_op jit(solution)/shard_map/ppermute | solution.py:12
  743.9 0.8 collective-permute-done.1
  744.7 0.5 convolution_bitcast_fusion
  745.2 2.0 copy.31
  747.3 0.0 reduce-scatter.12.cloned.1.call-start
  747.3 2.1 fusion.33
  749.5 0.0 reduce-scatter.12.cloned.1.call-update
  749.5 0.0 all-reduce.3.cloned.1.call-start
  749.5 195.9 %reduce-scatter.10.cloned.1.call-done = f32[160,64]{1,0:T(8,128)} async-done(((f32[5120,64]{1,0:T(8,128)}), f32[160,64]{1,0:T(8,128)}) %reduce-scatter.10.cloned.1.call-update) | async-done | bytes 40976
  945.4 1.6 copy.32
  947.0 225.5 %reduce-scatter.12.cloned.1.call-done = f32[160,64]{1,0:T(8,128)} async-done(((f32[5120,64]{1,0:T(8,128)}), f32[160,64]{1,0:T(8,128)}) %reduce-scatter.12.cloned.1.call-update) | async-done | bytes 40976
  1172.5 1.6 copy.34
  1174.2 86.4 %all-reduce.3.cloned.1.call-done = (f32[64,160]{1,0:T(8,128)}, f32[160,64]{0,1:T(8,128)}) async-done(((f32[64,160]{1,0:T(8,128)}, f32[160,64]{0,1:T(8,128)}), (f32[64,160]{1,0:T(8,128)}, f32[160,64]{0,1:T(8,128)})) %all-reduce.3.cloned.1.call-update) | async-done | bytes 81936 | tf_op jit(solution)/shard_map/psum | solution.py:132
  1260.6 1.5 copy.47
  1262.0 1.5 copy.48
  (22 shorter events, 0.1 us)
Async XLA Ops:
  7.2 9.1 copy-start
  7.2 9.1 copy-start.6
  7.2 9.1 copy-start.7
  7.2 41.4 %all-gather.12.cloned.1.call-start = ((), (), s32[]{:S(2)}) async-start(), calls=%async_computation.6 | async-start | bytes 1474560 | tf_op jit(solution)/shard_map/all_gather | solution.py:104
  7.9 12.8 %copy-start.2 = (bf16[64,5120]{1,0:T(8,128)(2,1)S(1)}, bf16[64,5120]{1,0:T(8,128)(2,1)}, u32[]{:S(2)}) copy-start(bf16[64,5120]{1,0:T(8,128)(2,1)} %param.20) | copy-start | bytes 1966084
  7.9 12.8 %copy-start.3 = (bf16[64,5120]{1,0:T(8,128)(2,1)S(1)}, bf16[64,5120]{1,0:T(8,128)(2,1)}, u32[]{:S(2)}) copy-start(bf16[64,5120]{1,0:T(8,128)(2,1)} %param.24) | copy-start | bytes 1966084
  8.0 79.3 %all-gather.14.cloned.1.call-start = ((), (), s32[]{:S(2)}) async-start(), calls=%async_computation.7 | async-start | bytes 1474560 | tf_op jit(solution)/shard_map/all_gather | solution.py:105
  8.7 132.1 %all-gather.10.cloned.1.call-start = ((), (), s32[]{:S(2)}) async-start(), calls=%async_computation.5 | async-start | bytes 4423680 | tf_op jit(solution)/shard_map/all_gather | solution.py:103
  10.8 182.6 %all-gather.8.cloned.1.call-start = ((), (), s32[]{:S(2)}) async-start(), calls=%async_computation.4 | async-start | bytes 4423680 | tf_op jit(solution)/shard_map/all_gather | solution.py:102
  12.9 74.3 %copy-start.4 = (bf16[5120,64]{0,1:T(8,128)(2,1)S(1)}, bf16[5120,64]{0,1:T(8,128)(2,1)}, u32[]{:S(2)}) copy-start(bf16[5120,64]{0,1:T(8,128)(2,1)} %param.23) | copy-start | bytes 1966084
  12.9 476.8 %all-gather.6.cloned.1.call-start = ((), (), s32[]{:S(2)}) async-start(), calls=%async_computation.3 | async-start | bytes 21626880 | tf_op jit(solution)/shard_map/all_gather | solution.py:47
  16.6 4.2 collective-permute-start
  22.0 694.1 %reduce-scatter.8.cloned.1.call-start = ((), (), s32[]{:S(2)}) async-start(), calls=%async_computation.8 | async-start | bytes 1081344 | tf_op jit(solution)/shard_map/reduce_scatter | solution.py:57
  504.3 211.8 %copy-start.1 = (bf16[64,5120]{1,0:T(8,128)(2,1)S(1)}, bf16[64,5120]{1,0:T(8,128)(2,1)}, u32[]{:S(2)}) copy-start(bf16[64,5120]{1,0:T(8,128)(2,1)} %convolution_convert_fusion) | copy-start | bytes 1966084
  520.0 425.4 %reduce-scatter.10.cloned.1.call-start = ((), (), s32[]{:S(2)}) async-start(), calls=%async_computation.9 | async-start | bytes 2703360
  717.6 27.1 %collective-permute-start.1 = (f32[32,64]{1,0:T(8,128)S(1)}, f32[32,64]{1,0:T(8,128)S(1)}, u32[]{:S(2)}, u32[]{:S(2)}) collective-permute-start(f32[32,64]{1,0:T(8,128)S(1)} %constant_dynamic-slice_fusion), channel_id=1, source_target_pairs={{0,32},{32,0},{64,96},{96,64},{128,160},{160,128},{192,224},{224,1... | collective-permute-start | bytes 24584 | tf_op jit(solution)/shard_map/ppermute | solution.py:12
  744.7 2.6 copy-start.5
  747.3 425.3 %reduce-scatter.12.cloned.1.call-start = ((), (), s32[]{:S(2)}) async-start(), calls=%async_computation.10 | async-start | bytes 2703360
  749.5 511.1 %all-reduce.3.cloned.1.call-start = ((), (), s32[]{:S(2)}) async-start(), calls=%async_computation.11 | async-start | bytes 262144 | tf_op jit(solution)/shard_map/psum | solution.py:132
Sparse Core Ops, SparseCore 0:
  9.8 38.7 all-gather.11
  50.4 36.7 all-gather.13
  89.0 51.7 all-gather.9
  142.5 50.8 all-gather.7
  196.6 293.0 all-gather.5
  520.1 195.9 reduce-scatter.7
  747.4 197.9 reduce-scatter.9
  948.1 224.3 reduce-scatter.11
  1176.0 84.5 all-reduce.2
where the time goes:
time: 1270 us
  waiting for transfers between devices  1170 us (92%)
  matrix products  35.5 us (3%)
  starting transfers between devices  30 us (2%)
  between operations  14.7 us (1%)
  local copies, waits for them, and re-layouts  14.5 us (1%)
    unnamed x11, waiting for transfers between devices  423 us
    all_gather x1, waiting for transfers between devices, score_model(): lax.all_gather(own_stream, 'seq', axis=0, tiled=True)  292 us
    reduce_scatter x1, waiting for transfers between devices, score_model(): lax.psum_scatter(jnp.dot(flat_attended.astype(jnp.float32), mixed, precis...  196 us
    psum x1, waiting for transfers between devices, body(): grad_in, grad_out = lax.psum((grad_in, grad_out), 'mp')  86.4 us
    all_gather x1, waiting for transfers between devices, body(): lax.all_gather(real_qkv, 'mp', axis=0, tiled=True)  52.5 us
    all_gather x1, waiting for transfers between devices, body(): lax.all_gather(fake_qkv, 'mp', axis=0, tiled=True)  51 us
    all_gather x1, waiting for transfers between devices, body(): lax.all_gather(fake_proj, 'mp', axis=2, tiled=True)  38.6 us
    ppermute x2, starting transfers between devices, from_partner(): return lax.ppermute(value, axis, pairs)  29.6 us
  transfers between devices with their start and end apart: 11, of which 11 were waited for; matrix products, arithmetic and copies ran while one was open for 1% of the time, Pallas kernels for 0%

commit v1 on v0

v1 whole, which is shorter than its diff:
```python
import functools
import math

import jax
import jax.numpy as jnp
from jax import lax
from jax.experimental import pallas as pl
from jax.experimental.pallas import tpu as pltpu
from jax.sharding import PartitionSpec as P

MESH = pl.DeviceIdType.MESH
F32 = jnp.float32
BF16 = jnp.bfloat16
NN = (((1,), (0,)), ((), ()))
NT = (((1,), (1,)), ((), ()))
HIGH = lax.Precision.HIGHEST
SCORE_SCALE = math.log2(math.e) / math.sqrt(128.0)
LOSS_SCALE = 1.0 / math.sqrt(8192.0)


def mm(a, b, dims=NN, precision=None):
    return lax.dot_general(a, b, dims, precision=precision, preferred_element_type=F32)


def lanes(shape):
    return lax.broadcasted_iota(jnp.int32, shape, len(shape) - 1)


def roll(value, shift):
    return pltpu.roll(value, shift, 1)


def fold(square):
    return jnp.concatenate([square[0:32], square[32:64]], axis=1)


def kernel(
    steps,
    noise_gen,
    noise_add,
    gen_in,
    gen_out,
    real_in,
    real_qkv,
    real_proj,
    real_head,
    fake_in,
    fake_qkv,
    fake_proj,
    fake_head,
    dmd_out,
    gin_out,
    gout_out,
    gin_v,
    gout_v,
    emb_v,
    head_v,
    qkv_v,
    proj_v,
    embs_v,
    heads_v,
    job_send,
    job_recv,
    ac,
    msg,
    msg_r,
    tok,
    noi,
    keys_t,
    vals,
    hid,
    dsil,
    vel,
    vel_r,
    sca,
    gpart,
    grecv,
    fin,
    load_sem,
    job_ssem,
    job_rsem,
    z_ssem,
    z_rsem,
    ac_ssem,
    ac_rsem,
    core_ssem,
    core_rsem,
    tokz_ssem,
    tokz_rsem,
    tok_ssem,
    tok_rsem,
    noi_ssem,
    noi_rsem,
    sca_ssem,
    sca_rsem,
    g_ssem,
    g_rsem,
):
    mp = lax.axis_index("mp")
    seq = lax.axis_index("seq")
    core = mp % 2
    zlo = mp // 2
    x = seq // 8
    zhi = (seq // 4) % 2
    y = seq % 4
    me_p = x * 4 + y

    def dev(x_, y_, zhi_, zlo_, core_):
        return (zlo_ * 2 + core_, x_ * 8 + zhi_ * 4 + y_)

    def plane_dev(k):
        return dev((x + k // 4) % 4, (y + k % 4) % 4, zhi, zlo, core)

    partner = dev(x, y, zhi, zlo, 1 - core)
    across = dev(x, y, 1 - zhi, zlo, core)

    def rc(src, dst, ssem, rsem, device):
        return pltpu.make_async_remote_copy(
            src_ref=src, dst_ref=dst, send_sem=ssem, recv_sem=rsem, device_id=device, device_id_type=MESH
        )

    def to_plane(src, dst, ssem, rsem):
        def send(k, carry):
            rc(src, dst, ssem, rsem, plane_dev(k)).start()
            return carry

        lax.fori_loop(1, 16, send, 0)

    def got(ref, rsem):
        rc(ref, ref, rsem, rsem, partner).wait_recv()

    def sent(ref, ssem):
        rc(ref, ref, ssem, ssem, partner).wait_send()

    row = pl.ds(pl.multiple_of(mp * 640, 128), 640)
    loads = [
        pltpu.make_async_copy(real_in.at[:, row], embs_v.at[0], load_sem.at[0]),
        pltpu.make_async_copy(real_qkv, qkv_v.at[0], load_sem.at[1]),
        pltpu.make_async_copy(real_head.at[:, row], heads_v.at[0], load_sem.at[2]),
        pltpu.make_async_copy(real_proj, proj_v.at[0], load_sem.at[3]),
        pltpu.make_async_copy(fake_in.at[:, row], embs_v.at[1], load_sem.at[4]),
        pltpu.make_async_copy(fake_qkv, qkv_v.at[1], load_sem.at[5]),
        pltpu.make_async_copy(fake_head.at[:, row], heads_v.at[1], load_sem.at[6]),
        pltpu.make_async_copy(fake_proj, proj_v.at[1], load_sem.at[7]),
        pltpu.make_async_copy(gen_in, gin_v, load_sem.at[8]),
        pltpu.make_async_copy(gen_out, gout_v, load_sem.at[9]),
    ]
    for load in loads:
        load.start()

    @pl.when(core == 0)
    def _():
        pltpu.make_async_copy(real_in, emb_v, load_sem.at[10]).start()
        pltpu.make_async_copy(real_head, head_v, load_sem.at[11]).start()

    @pl.when(core == 1)
    def _():
        pltpu.make_async_copy(fake_in, emb_v, load_sem.at[10]).start()
        pltpu.make_async_copy(fake_head, head_v, load_sem.at[11]).start()

    barrier = pltpu.get_barrier_semaphore()

    def greet(device):
        pl.semaphore_signal(barrier, inc=1, device_id=device, device_id_type=MESH)

    def greet_plane(k, carry):
        greet(plane_dev(k))
        return carry

    def greet_mp(k, carry):
        greet(((mp + k) % 8, seq))
        return carry

    def greet_across(k, carry):
        greet(dev(x, y, 1 - zhi, k, core))
        return carry

    lax.fori_loop(1, 8, greet_mp, 0)
    lax.fori_loop(0, 4, greet_across, 0)
    lax.fori_loop(1, 16, greet_plane, 0)

    for m in range(2):
        for k in range(4):
            loads[4 * m + k].wait()
        for c in range(3):
            job_send[2 * m + c // 2, :, (c % 2) * 128 : (c % 2) * 128 + 128] = mm(embs_v[m], qkv_v[m, c]).astype(BF16)
        job_send[2 * m + 1, :, 128:256] = mm(heads_v[m], proj_v[m], NT).astype(BF16)

    level = steps[zlo].astype(F32) / 1000.0
    loads[8].wait()
    loads[9].wait()
    own_noise = noise_gen[...]
    clean = own_noise.astype(F32)
    for c in range(5):
        cols = slice(c * 1024, c * 1024 + 1024)
        u = mm(own_noise, gin_v[:, cols])
        hidden = (u * jax.nn.sigmoid(u)).astype(BF16)
        clean = clean + mm(hidden, gout_v[:, cols], NT)
    noised = (1.0 - level) * clean + level * noise_add[...].astype(F32)
    msg[...] = jnp.concatenate([noised, own_noise.astype(F32)], axis=1).astype(BF16)

    pl.semaphore_wait(barrier, 26)

    for m in range(2):
        for t in range(2):

            @pl.when(jnp.logical_not((zlo == 1 + t) & (core == m)))
            def _(m=m, t=t):
                rc(
                    job_send.at[2 * m + t],
                    job_recv.at[mp],
                    job_ssem.at[2 * m + t],
                    job_rsem.at[mp],
                    dev(x, y, zhi, 1 + t, m),
                ).start()

    rc(msg, msg_r, core_ssem.at[0], core_rsem.at[0], partner).start()
    got(msg_r, core_rsem.at[0])
    left = lanes((32, 128)) < 64
    mine = msg[...].astype(F32)
    other = msg_r[...].astype(F32)
    half0 = jnp.where(core == 0, mine, other)
    half1 = jnp.where(core == 0, other, mine)
    own_tok = jnp.where(left, half0, roll(half1, 64))
    tok[zhi, me_p] = own_tok.astype(BF16)
    noi[me_p] = jnp.where(left, roll(half0, 64), half1).astype(BF16)
    own_ref = tok.at[zhi, me_p]
    rc(own_ref, own_ref, tokz_ssem, tokz_rsem, across).start()
    to_plane(own_ref, own_ref, tok_ssem, tok_rsem)
    xtok = jnp.concatenate([own_tok[:, 0:64], own_tok[:, 64:128]], axis=0)
    xfold = jnp.concatenate([xtok[:, 0:32], xtok[:, 32:64]], axis=0).astype(BF16)
    xtok = xtok.astype(BF16)

    pltpu.make_async_copy(real_in, emb_v, load_sem.at[10]).wait()
    pltpu.make_async_copy(real_head, head_v, load_sem.at[11]).wait()
    direct = mm(emb_v[...], head_v[...], NT)
    vel[...] = mm(xtok.astype(F32), direct, precision=HIGH)

    t_here = zlo - 1
    slot_here = zhi * 2 + t_here

    @pl.when((zlo == 1) | (zlo == 2))
    def _():
        total = job_send[core * 2 + t_here].astype(F32)
        for src in range(8):

            @pl.when(src != mp)
            def _(src=src):
                got(job_recv.at[src], job_rsem.at[src])

            @pl.when(src == mp)
            def _(src=src):
                job_recv[src] = jnp.zeros((64, 256), BF16)

            total = total + job_recv[src].astype(F32)
        scale = jnp.where(t_here == 0, SCORE_SCALE, 1.0).astype(F32)
        square = mm(total[:, 0:128], total[:, 128:256], NT, HIGH) * scale
        ac[me_p, slot_here] = fold(square).astype(BF16)
        piece = ac.at[me_p, slot_here]

        def spread(k, carry):
            z = (zhi * 4 + zlo + k) % 8
            rc(piece, piece, z_ssem, z_rsem.at[slot_here], dev(x, y, z // 4, z % 4, core)).start()
            return carry

        lax.fori_loop(1, 8, spread, 0)

    far_ref = tok.at[1 - zhi, me_p]
    got(far_ref, tokz_rsem)
    to_plane(far_ref, far_ref, tok_ssem, tok_rsem)

    for order in range(4):
        group = zhi if order < 2 else 1 - zhi
        slot = group * 2 + order % 2
        piece = ac.at[me_p, slot]

        @pl.when(jnp.logical_not((group == zhi) & (zlo == 1 + order % 2)))
        def _(piece=piece, slot=slot):
            got(piece, z_rsem.at[slot])

        to_plane(piece, piece, ac_ssem, ac_rsem.at[me_p])

    noi_ref = noi.at[me_p]
    to_plane(noi_ref, noi_ref, noi_ssem, noi_rsem)

    got(tok.at[0:2, 0:15], tok_rsem)
    for g in range(2):
        block = tok[g].reshape(512, 128).astype(F32)
        flipped = block.T.astype(BF16)
        keys_t[:, g * 512 : g * 512 + 512] = flipped[0:64]
        keys_t[:, 1024 + g * 512 : 1024 + g * 512 + 512] = flipped[64:128]
        near = lanes((512, 128)) < 64
        vals[g * 512 : g * 512 + 512, :] = jnp.where(near, block, 1.0).astype(BF16)
        vals[1024 + g * 512 : 1024 + g * 512 + 512, :] = jnp.where(near, roll(block, 64), 1.0).astype(BF16)

    def attend(b, acc):
        spots = []
        for e in range(2):
            k = 2 * b + e
            spot = ((x + k // 4) % 4) * 4 + (y + k % 4) % 4
            spots.append(spot)

            @pl.when(k > 0)
            def _(spot=spot):
                got(ac.at[spot], ac_rsem.at[spot])

        mats = jnp.concatenate([ac[spots[e], 2 * g] for e in range(2) for g in range(2)], axis=1)
        both = mm(xfold, mats)
        queries = jnp.concatenate(
            [
                both[0:64, i * 128 : i * 128 + 64] + both[64:128, i * 128 + 64 : i * 128 + 128]
                for i in range(4)
            ],
            axis=0,
        ).astype(BF16)
        scores = mm(queries, keys_t[...])
        top = jnp.max(scores, axis=1, keepdims=True)
        weights = jnp.exp2(scores - top).astype(BF16)
        mixed = mm(weights, vals[...])
        heads = (mixed[:, 0:64] / mixed[:, 64:128]).astype(BF16)
        for i in range(4):
            part = heads[i * 64 : i * 64 + 64]
            folded = jnp.concatenate([part[:, 0:32], part[:, 32:64]], axis=0)
            acc = acc + mm(folded, ac[spots[i // 2], 2 * (i % 2) + 1])
        return acc

    acc = lax.fori_loop(0, 8, attend, jnp.zeros((128, 128), F32))
    total_vel = vel[...] + acc[0:64, 0:64] + acc[64:128, 64:128]
    vel_fold = jnp.concatenate([total_vel[0:32], total_vel[32:64]], axis=1)
    sca_f = vel_fold
    fin[0:32, :] = sca_f
    rc(fin.at[0:32], vel_r, core_ssem.at[1], core_rsem.at[1], partner).start()

    got(noi.at[0:15], noi_rsem)
    col0 = 160 * (x * 8 + core * 4 + y)
    base = pl.ds(pl.multiple_of((col0 // 128) * 128, 128), 256)
    shift = 256 - 32 * y
    gin_s = pltpu.roll(gin_v[:, base].astype(F32), shift, 1).astype(BF16)
    gout_s = pltpu.roll(gout_v[:, base].astype(F32), shift, 1).astype(BF16)
    zeros = jnp.zeros((64, 256), BF16)
    noise_rows = noi[...].reshape(512, 128)
    for h in range(2):
        weight = jnp.concatenate([gin_s, zeros] if h == 0 else [zeros, gin_s], axis=0)
        u = mm(noise_rows, weight)
        sig = jax.nn.sigmoid(u)
        hid[h] = (u * sig).astype(BF16)
        dsil[h] = sig * (1.0 + u * (1.0 - sig))
    noise_t = noise_rows.astype(F32).T.astype(BF16)

    got(vel_r, core_rsem.at[1])
    sign = jnp.where(core == 0, 1.0, -1.0).astype(F32)
    dmd = level * (sign * (vel_fold - vel_r[...]))
    dmd_out[...] = jnp.where(core == 0, dmd[:, 0:64], dmd[:, 64:128])
    sca[me_p] = (dmd * LOSS_SCALE).astype(BF16)
    sca_ref = sca.at[me_p]
    to_plane(sca_ref, sca_ref, sca_ssem, sca_rsem)
    got(sca.at[0:15], sca_rsem)

    scaled_rows = sca[...].reshape(512, 128)
    scaled_t = scaled_rows.astype(F32).T.astype(BF16)
    grad_in = jnp.zeros((64, 256), F32)
    grad_out = jnp.zeros((64, 256), F32)
    for h in range(2):
        grad_out = grad_out + mm(scaled_t[h * 64 : h * 64 + 64], hid[h])
        weight = jnp.concatenate([gout_s, zeros] if h == 0 else [zeros, gout_s], axis=0)
        pre = (mm(scaled_rows, weight) * dsil[h]).astype(BF16)
        grad_in = grad_in + mm(noise_t[h * 64 : h * 64 + 64], pre)
    grads = jnp.concatenate([grad_in, grad_out], axis=0)
    lane32 = lanes((32, 128))
    rest = grads[0:32, 128:256]
    for i in range(1, 4):
        rest = jnp.where(lane32 < 32 * i, rest, roll(grads[32 * i : 32 * i + 32, 128:256], 32 * i))
    gpart[0:128, :] = grads[:, 0:128].astype(BF16)
    gpart[128:160, :] = rest.astype(BF16)

    zme = zhi * 4 + zlo
    for k in range(4):

        @pl.when(jnp.logical_not((zhi == core) & (zlo == k)))
        def _(k=k):
            rc(gpart, grecv.at[zme], g_ssem.at[k], g_rsem.at[zme], dev(x, y, core, k, core)).start()

    @pl.when(zhi == core)
    def _():
        total = gpart[...].astype(F32)
        for src in range(8):

            @pl.when(src != zme)
            def _(src=src):
                got(grecv.at[src], g_rsem.at[src])

            @pl.when(src == zme)
            def _(src=src):
                grecv[src] = jnp.zeros((160, 128), BF16)

            total = total + grecv[src].astype(F32)
        fin[32:192, :] = total
        rc(fin.at[32:192], fin.at[32:192], core_ssem.at[2], core_rsem.at[2], partner).start()

    @pl.when(zhi != core)
    def _():
        got(fin.at[32:192], core_rsem.at[2])

    gin_out[:, 0:128] = fin[32:96, :]
    gout_out[:, 0:128] = fin[96:160, :]
    tail = fin[160:192, :]
    for i in range(4):
        ref = gin_out if i < 2 else gout_out
        piece = tail if i == 0 else roll(tail, 128 - 32 * i)
        ref[(i % 2) * 32 : (i % 2) * 32 + 32, 128:160] = piece[:, 0:32]

    for m in range(2):
        for t in range(2):

            @pl.when(jnp.logical_not((zlo == 1 + t) & (core == m)))
            def _(m=m, t=t):
                sent(job_send.at[2 * m + t], job_ssem.at[2 * m + t])

    @pl.when((zlo == 1) | (zlo == 2))
    def _():
        sent(noi.at[0:7], z_ssem)

    for k in range(4):

        @pl.when(jnp.logical_not((zhi == core) & (zlo == k)))
        def _(k=k):
            sent(gpart, g_ssem.at[k])

    @pl.when(zhi == core)
    def _():
        sent(fin.at[32:192], core_ssem.at[2])

    sent(msg, core_ssem.at[0])
    sent(fin.at[0:32], core_ssem.at[1])
    sent(own_ref, tokz_ssem)
    sent(tok.at[0:2, 0:15], tok_ssem)
    sent(ac.at[0:15], ac_ssem)
    sent(noi.at[0:15], noi_ssem)
    sent(sca.at[0:15], sca_ssem)


def body(
    noise_gen,
    noise_add,
    steps_t,
    gen_in,
    gen_out,
    real_in,
    real_qkv,
    real_proj,
    real_head,
    fake_in,
    fake_qkv,
    fake_proj,
    fake_head,
):
    def table(qkv):
        return qkv.transpose(1, 2, 0, 3).reshape(3, 640, 128)

    vmem = pl.BlockSpec(memory_space=pltpu.VMEM)
    hbm = pl.BlockSpec(memory_space=pl.ANY)
    dma = pltpu.SemaphoreType.DMA
    dmd, grad_in, grad_out = pl.pallas_call(
        kernel,
        out_shape=(
            jax.ShapeDtypeStruct((32, 64), F32),
            jax.ShapeDtypeStruct((64, 160), F32),
            jax.ShapeDtypeStruct((64, 160), F32),
        ),
        in_specs=[pl.BlockSpec(memory_space=pltpu.SMEM), vmem, vmem] + [hbm] * 10,
        out_specs=(vmem, vmem, vmem),
        scratch_shapes=[
            pltpu.VMEM((64, 5120), BF16),
            pltpu.VMEM((64, 5120), BF16),
            pltpu.VMEM((64, 5120), BF16),
            pltpu.VMEM((64, 5120), BF16),
            pltpu.VMEM((2, 3, 640, 128), BF16),
            pltpu.VMEM((2, 128, 640), BF16),
            pltpu.VMEM((2, 64, 640), BF16),
            pltpu.VMEM((2, 64, 640), BF16),
            pltpu.VMEM((4, 64, 256), BF16),
            pltpu.VMEM((8, 64, 256), BF16),
            pltpu.VMEM((16, 4, 32, 128), BF16),
            pltpu.VMEM((32, 128), BF16),
            pltpu.VMEM((32, 128), BF16),
            pltpu.VMEM((2, 16, 32, 128), BF16),
            pltpu.VMEM((16, 32, 128), BF16),
            pltpu.VMEM((64, 2048), BF16),
            pltpu.VMEM((2048, 128), BF16),
            pltpu.VMEM((2, 512, 256), BF16),
            pltpu.VMEM((2, 512, 256), F32),
            pltpu.VMEM((64, 64), F32),
            pltpu.VMEM((32, 128), F32),
            pltpu.VMEM((16, 32, 128), BF16),
            pltpu.VMEM((160, 128), BF16),
            pltpu.VMEM((8, 160, 128), BF16),
            pltpu.VMEM((192, 128), F32),
            dma((12,)),
            dma((4,)),
            dma((8,)),
            dma,
            dma((4,)),
            dma,
            dma((16,)),
            dma((3,)),
            dma((3,)),
            dma,
            dma,
            dma,
            dma,
            dma,
            dma,
            dma,
            dma,
            dma((4,)),
            dma((8,)),
        ],
        compiler_params=pltpu.CompilerParams(
            collective_id=0, has_side_effects=True, vmem_limit_bytes=48 * 1024 * 1024
        ),
    )(
        steps_t,
        noise_gen[0],
        noise_add[0],
        gen_in,
        gen_out.T,
        real_in,
        table(real_qkv),
        real_proj[0],
        real_head.T,
        fake_in,
        table(fake_qkv),
        fake_proj[0],
        fake_head.T,
    )
    return dmd[None], grad_in, grad_out.T


def solution(mesh):
    return jax.shard_map(
        body,
        mesh=mesh,
        in_specs=(
            P("mp", "seq", None),
            P("mp", "seq", None),
            P(),
            P(),
            P(),
            P(),
            P("mp", None, "seq", None),
            P("seq", None, "mp"),
            P(),
            P(),
            P("mp", None, "seq", None),
            P("seq", None, "mp"),
            P(),
        ),
        out_specs=(P("mp", "seq", None), P(None, "seq"), P("seq", None)),
        check_vma=False,
    )
```

time: 1270 us -> 69.1 us (0.05)
  waiting for transfers between devices: 1170 us -> 0 us
  Pallas kernels: 0 us -> 54.9 us
  matrix products: 35.5 us -> 0 us
  starting transfers between devices: 30 us -> 0 us
  between operations: 14.7 us -> 0.68 us
    all_gather x5 -> x0, waiting for transfers between devices: 461 us -> none  [the longest x1 292 us: score_model(): lax.all_gather(own_stream, 'seq', axis=0, tiled=True)]
    unnamed x11 -> x0, waiting for transfers between devices: 423 us -> none
    reduce_scatter x1 -> x0, waiting for transfers between devices: 196 us -> none  [score_model(): lax.psum_scatter(jnp.dot(flat_attended.astype(jnp.float32), mixed, precis...]
    psum x1 -> x0, waiting for transfers between devices: 86.4 us -> none  [body(): grad_in, grad_out = lax.psum((grad_in, grad_out), 'mp')]
    pallas_call x0 -> x1, Pallas kernels: none -> 54.9 us  [body(): pl.pallas_call(kernel, out_shape=(jax.ShapeDtypeStruct((32, 64), F32), ja...]
    dot_general x16 -> x0, matrix products: 33.3 us -> none  [the longest x1 13.6 us: score_model(): jnp.dot(lax.all_gather(own_stream, 'seq', axis=0, tiled=True), flat_table...]
    ppermute x2 -> x0, starting transfers between devices: 29.6 us -> none  [from_partner(): return lax.ppermute(value, axis, pairs)]
  transfers between devices with their start and end apart: 11 -> 0, of which waited for: 11 -> 0; matrix products, arithmetic and copies ran while one was open for 1% -> 0% of each run, Pallas kernels for 0% -> 0%
where the time goes in v1:
time: 69.1 us; the launch traced here: 68.6 us
  Pallas kernels  54.9 us (79%)
  local copies, waits for them, and re-layouts  13 us (19%)
    pallas_call x1, Pallas kernels, body(): pl.pallas_call(kernel, out_shape=(jax.ShapeDtypeStruct((32, 64), F32), ja...  54.9 us
    unnamed x29, local copies, waits for them, and re-layouts  13 us

profile of v1, /device:TPU:1, one launch (start us, length us, event | category | flops | bytes accessed | tf_op | source)
XLA Modules:
  0.0 68.6 jit_solution(5483979343785234133)
XLA Ops:
  0.6 0.0 copy-start.11
  0.6 0.0 copy-start.10
  0.7 0.0 copy-start.12
  0.7 0.7 copy-done.11
  1.3 0.0 copy-done.10
  1.4 0.0 copy-done.12
  1.4 0.0 copy-start
  1.4 1.1 %copy-done = bf16[64,5120]{1,0:T(8,128)(2,1)S(1)} copy-done((bf16[64,5120]{1,0:T(8,128)(2,1)S(1)}, bf16[64,5120]{1,0:T(8,128)(2,1)}, u32[]{:S(2)}) %copy-start) | copy-done | bytes 655384
  2.4 0.0 copy-start.1
  2.4 1.1 %copy-done.1 = bf16[5120,64]{0,1:T(8,128)(2,1)S(1)} copy-done((bf16[5120,64]{0,1:T(8,128)(2,1)S(1)}, bf16[5120,64]{0,1:T(8,128)(2,1)}, u32[]{:S(2)}) %copy-start.1) | copy-done | bytes 655384
  3.5 0.0 copy-start.2
  3.5 1.1 %copy-done.2 = bf16[64,5120]{1,0:T(8,128)(2,1)S(1)} copy-done((bf16[64,5120]{1,0:T(8,128)(2,1)S(1)}, bf16[64,5120]{1,0:T(8,128)(2,1)}, u32[]{:S(2)}) %copy-start.2) | copy-done | bytes 655384
  4.6 0.0 copy-start.3
  4.6 1.1 %copy-done.3 = bf16[5120,64]{0,1:T(8,128)(2,1)S(1)} copy-done((bf16[5120,64]{0,1:T(8,128)(2,1)S(1)}, bf16[5120,64]{0,1:T(8,128)(2,1)}, u32[]{:S(2)}) %copy-start.3) | copy-done | bytes 655384
  5.7 0.0 copy-start.4
  5.7 1.1 %copy-done.4 = bf16[64,5120]{1,0:T(8,128)(2,1)S(1)} copy-done((bf16[64,5120]{1,0:T(8,128)(2,1)S(1)}, bf16[64,5120]{1,0:T(8,128)(2,1)}, u32[]{:S(2)}) %copy-start.4) | copy-done | bytes 655384
  6.8 0.0 copy-start.5
  6.8 1.1 %copy-done.5 = bf16[5120,64]{0,1:T(8,128)(2,1)S(1)} copy-done((bf16[5120,64]{0,1:T(8,128)(2,1)S(1)}, bf16[5120,64]{0,1:T(8,128)(2,1)}, u32[]{:S(2)}) %copy-start.5) | copy-done | bytes 655384
  7.9 0.0 copy-start.6
  7.9 1.0 %copy-done.6 = bf16[640,3,1,128]{3,0,2,1:T(8,128)(2,1)S(1)} copy-done((bf16[640,3,1,128]{3,0,2,1:T(8,128)(2,1)S(1)}, bf16[640,3,1,128]{3,0,2,1:T(8,128)(2,1)}, u32[]{:S(2)}) %copy-start.6) | copy-done | bytes 491544
  8.9 0.0 copy-start.7
  8.9 1.0 %copy-done.7 = bf16[640,3,1,128]{3,0,2,1:T(8,128)(2,1)S(1)} copy-done((bf16[640,3,1,128]{3,0,2,1:T(8,128)(2,1)S(1)}, bf16[640,3,1,128]{3,0,2,1:T(8,128)(2,1)}, u32[]{:S(2)}) %copy-start.7) | copy-done | bytes 491544
  9.9 0.0 copy-start.8
  9.9 0.9 %copy-done.8 = bf16[1,128,640]{2,1,0:T(8,128)(2,1)S(1)} copy-done((bf16[1,128,640]{2,1,0:T(8,128)(2,1)S(1)}, bf16[1,128,640]{2,1,0:T(8,128)(2,1)}, u32[]{:S(2)}) %copy-start.8) | copy-done | bytes 163864
  10.9 0.0 copy-start.9
  10.9 0.9 %copy-done.9 = bf16[1,128,640]{2,1,0:T(8,128)(2,1)S(1)} copy-done((bf16[1,128,640]{2,1,0:T(8,128)(2,1)S(1)}, bf16[1,128,640]{2,1,0:T(8,128)(2,1)}, u32[]{:S(2)}) %copy-start.9) | copy-done | bytes 163864
  11.8 54.9 %shard_map.148 = (f32[32,64]{1,0:T(8,128)S(1)}, f32[64,160]{1,0:T(8,128)S(1)}, f32[64,160]{1,0:T(8,128)S(1)}) custom-call(s32[4]{0:T(128)S(1)} %copy-done.12, bf16[32,64]{1,0:T(8,128)(2,1)S(1)} %bitcast.28, bf16[32,64]{1,0:T(8,128)(2,1)S(1)} %bitcast.29, bf16[64,5120]{1,0:T(8,128)(2,1)S(1)} %copy-done, bf16[64,5120]{1,0:T(8,128)(2,1)S(1)} %bitcast.19, ...), custom_call_target="tpu_custom_call" | custom-call | tf_op jit(solution)/shard_map/pallas_call | solution.py:463
  66.7 0.6 copy.21
  67.3 0.6 copy.22
  68.0 0.6 copy.23
Async XLA Ops:
  0.6 0.7 %copy-start.11 = (bf16[1,32,64]{2,1,0:T(8,128)(2,1)S(1)}, bf16[1,32,64]{2,1,0:T(8,128)(2,1)}, u32[]{:S(2)}) copy-start(bf16[1,32,64]{2,1,0:T(8,128)(2,1)} %param.14) | copy-start | bytes 12292
  0.6 0.7 %copy-start.10 = (bf16[1,32,64]{2,1,0:T(8,128)(2,1)S(1)}, bf16[1,32,64]{2,1,0:T(8,128)(2,1)}, u32[]{:S(2)}) copy-start(bf16[1,32,64]{2,1,0:T(8,128)(2,1)} %param.13) | copy-start | bytes 12292
  0.7 0.7 %copy-start.12 = (s32[4]{0:T(128)S(1)}, s32[4]{0:T(128)}, u32[]{:S(2)}) copy-start(s32[4]{0:T(128)} %steps.1) | copy-start | bytes 52
  1.4 1.1 %copy-start = (bf16[64,5120]{1,0:T(8,128)(2,1)S(1)}, bf16[64,5120]{1,0:T(8,128)(2,1)}, u32[]{:S(2)}) copy-start(bf16[64,5120]{1,0:T(8,128)(2,1)} %gen_in.1) | copy-start | bytes 1966084
  2.4 1.1 %copy-start.1 = (bf16[5120,64]{0,1:T(8,128)(2,1)S(1)}, bf16[5120,64]{0,1:T(8,128)(2,1)}, u32[]{:S(2)}) copy-start(bf16[5120,64]{0,1:T(8,128)(2,1)} %param.17) | copy-start | bytes 1966084
  3.5 1.1 %copy-start.2 = (bf16[64,5120]{1,0:T(8,128)(2,1)S(1)}, bf16[64,5120]{1,0:T(8,128)(2,1)}, u32[]{:S(2)}) copy-start(bf16[64,5120]{1,0:T(8,128)(2,1)} %real_in.1) | copy-start | bytes 1966084
  4.6 1.1 %copy-start.3 = (bf16[5120,64]{0,1:T(8,128)(2,1)S(1)}, bf16[5120,64]{0,1:T(8,128)(2,1)}, u32[]{:S(2)}) copy-start(bf16[5120,64]{0,1:T(8,128)(2,1)} %param.21) | copy-start | bytes 1966084
  5.7 1.1 %copy-start.4 = (bf16[64,5120]{1,0:T(8,128)(2,1)S(1)}, bf16[64,5120]{1,0:T(8,128)(2,1)}, u32[]{:S(2)}) copy-start(bf16[64,5120]{1,0:T(8,128)(2,1)} %fake_in.1) | copy-start | bytes 1966084
  6.8 1.1 %copy-start.5 = (bf16[5120,64]{0,1:T(8,128)(2,1)S(1)}, bf16[5120,64]{0,1:T(8,128)(2,1)}, u32[]{:S(2)}) copy-start(bf16[5120,64]{0,1:T(8,128)(2,1)} %param.25) | copy-start | bytes 1966084
  7.9 1.0 %copy-start.6 = (bf16[640,3,1,128]{3,0,2,1:T(8,128)(2,1)S(1)}, bf16[640,3,1,128]{3,0,2,1:T(8,128)(2,1)}, u32[]{:S(2)}) copy-start(bf16[640,3,1,128]{3,0,2,1:T(8,128)(2,1)} %param.19) | copy-start | bytes 1474564
  8.9 1.0 %copy-start.7 = (bf16[640,3,1,128]{3,0,2,1:T(8,128)(2,1)S(1)}, bf16[640,3,1,128]{3,0,2,1:T(8,128)(2,1)}, u32[]{:S(2)}) copy-start(bf16[640,3,1,128]{3,0,2,1:T(8,128)(2,1)} %param.23) | copy-start | bytes 1474564
  9.9 0.9 %copy-start.8 = (bf16[1,128,640]{2,1,0:T(8,128)(2,1)S(1)}, bf16[1,128,640]{2,1,0:T(8,128)(2,1)}, u32[]{:S(2)}) copy-start(bf16[1,128,640]{2,1,0:T(8,128)(2,1)} %param.20) | copy-start | bytes 491524
  10.9 0.9 %copy-start.9 = (bf16[1,128,640]{2,1,0:T(8,128)(2,1)S(1)}, bf16[1,128,640]{2,1,0:T(8,128)(2,1)}, u32[]{:S(2)}) copy-start(bf16[1,128,640]{2,1,0:T(8,128)(2,1)} %param.24) | copy-start | bytes 491524

commit v2 on v1

--- a/solution.py
+++ b/solution.py
@@ -48,9 +48,10 @@
     fake_qkv,
     fake_proj,
     fake_head,
-    dmd_out,
-    gin_out,
-    gout_out,
+    fin,
+    steps_s,
+    ngen_v,
+    nadd_v,
     gin_v,
     gout_v,
     emb_v,
@@ -66,8 +67,9 @@
     msg_r,
     tok,
     noi,
-    keys_t,
-    vals,
+    keys,
+    vals_t,
+    scores,
     hid,
     dsil,
     vel,
@@ -75,7 +77,6 @@
     sca,
     gpart,
     grecv,
-    fin,
     load_sem,
     job_ssem,
     job_rsem,
@@ -144,6 +145,9 @@
         pltpu.make_async_copy(fake_proj, proj_v.at[1], load_sem.at[7]),
         pltpu.make_async_copy(gen_in, gin_v, load_sem.at[8]),
         pltpu.make_async_copy(gen_out, gout_v, load_sem.at[9]),
+        pltpu.make_async_copy(noise_gen, ngen_v, load_sem.at[12]),
+        pltpu.make_async_copy(noise_add, nadd_v, load_sem.at[13]),
+        pltpu.make_async_copy(steps, steps_s, load_sem.at[14]),
     ]
     for load in loads:
         load.start()
@@ -175,9 +179,9 @@
         greet(dev(x, y, 1 - zhi, k, core))
         return carry
 
-    lax.fori_loop(1, 8, greet_mp, 0)
     lax.fori_loop(0, 4, greet_across, 0)
     lax.fori_loop(1, 16, greet_plane, 0)
+    lax.fori_loop(1, 8, greet_mp, 0)
 
     for m in range(2):
         for k in range(4):
@@ -186,17 +190,17 @@
             job_send[2 * m + c // 2, :, (c % 2) * 128 : (c % 2) * 128 + 128] = mm(embs_v[m], qkv_v[m, c]).astype(BF16)
         job_send[2 * m + 1, :, 128:256] = mm(heads_v[m], proj_v[m], NT).astype(BF16)
 
-    level = steps[zlo].astype(F32) / 1000.0
-    loads[8].wait()
-    loads[9].wait()
-    own_noise = noise_gen[...]
+    for k in range(8, 13):
+        loads[k].wait()
+    level = steps_s[zlo].astype(F32) / 1000.0
+    own_noise = ngen_v[...]
     clean = own_noise.astype(F32)
     for c in range(5):
         cols = slice(c * 1024, c * 1024 + 1024)
         u = mm(own_noise, gin_v[:, cols])
         hidden = (u * jax.nn.sigmoid(u)).astype(BF16)
         clean = clean + mm(hidden, gout_v[:, cols], NT)
-    noised = (1.0 - level) * clean + level * noise_add[...].astype(F32)
+    noised = (1.0 - level) * clean + level * nadd_v[...].astype(F32)
     msg[...] = jnp.concatenate([noised, own_noise.astype(F32)], axis=1).astype(BF16)
 
     pl.semaphore_wait(barrier, 26)
@@ -228,13 +232,18 @@
     rc(own_ref, own_ref, tokz_ssem, tokz_rsem, across).start()
     to_plane(own_ref, own_ref, tok_ssem, tok_rsem)
     xtok = jnp.concatenate([own_tok[:, 0:64], own_tok[:, 64:128]], axis=0)
-    xfold = jnp.concatenate([xtok[:, 0:32], xtok[:, 32:64]], axis=0).astype(BF16)
-    xtok = xtok.astype(BF16)
+    xcol = xtok.T.astype(BF16)
+    xzero = jnp.zeros((64, 64), BF16)
+    xpair = jnp.concatenate(
+        [jnp.concatenate([xcol, xzero], axis=1), jnp.concatenate([xzero, xcol], axis=1)], axis=0
+    )
+    noi_ref = noi.at[me_p]
+    to_plane(noi_ref, noi_ref, noi_ssem, noi_rsem)
 
     pltpu.make_async_copy(real_in, emb_v, load_sem.at[10]).wait()
     pltpu.make_async_copy(real_head, head_v, load_sem.at[11]).wait()
     direct = mm(emb_v[...], head_v[...], NT)
-    vel[...] = mm(xtok.astype(F32), direct, precision=HIGH)
+    vel[...] = mm(xtok, direct, precision=HIGH)
 
     t_here = zlo - 1
     slot_here = zhi * 2 + t_here
@@ -254,7 +263,7 @@
 
             total = total + job_recv[src].astype(F32)
         scale = jnp.where(t_here == 0, SCORE_SCALE, 1.0).astype(F32)
-        square = mm(total[:, 0:128], total[:, 128:256], NT, HIGH) * scale
+        square = mm(total[:, 128:256], total[:, 0:128], NT, HIGH) * scale
         ac[me_p, slot_here] = fold(square).astype(BF16)
         piece = ac.at[me_p, slot_here]
 
@@ -269,63 +278,91 @@
     got(far_ref, tokz_rsem)
     to_plane(far_ref, far_ref, tok_ssem, tok_rsem)
 
+    upper = zlo // 2
     for order in range(4):
         group = zhi if order < 2 else 1 - zhi
-        slot = group * 2 + order % 2
+        t = upper if order in (0, 3) else 1 - upper
+        slot = group * 2 + t
         piece = ac.at[me_p, slot]
 
-        @pl.when(jnp.logical_not((group == zhi) & (zlo == 1 + order % 2)))
+        @pl.when(jnp.logical_not((group == zhi) & (zlo == 1 + t)))
         def _(piece=piece, slot=slot):
             got(piece, z_rsem.at[slot])
 
-        to_plane(piece, piece, ac_ssem, ac_rsem.at[me_p])
-
-    noi_ref = noi.at[me_p]
-    to_plane(noi_ref, noi_ref, noi_ssem, noi_rsem)
+        to_plane(piece, piece, ac_ssem, ac_rsem.at[group, me_p])
 
     got(tok.at[0:2, 0:15], tok_rsem)
     for g in range(2):
         block = tok[g].reshape(512, 128).astype(F32)
         flipped = block.T.astype(BF16)
-        keys_t[:, g * 512 : g * 512 + 512] = flipped[0:64]
-        keys_t[:, 1024 + g * 512 : 1024 + g * 512 + 512] = flipped[64:128]
-        near = lanes((512, 128)) < 64
-        vals[g * 512 : g * 512 + 512, :] = jnp.where(near, block, 1.0).astype(BF16)
-        vals[1024 + g * 512 : 1024 + g * 512 + 512, :] = jnp.where(near, roll(block, 64), 1.0).astype(BF16)
-
-    def attend(b, acc):
-        spots = []
-        for e in range(2):
-            k = 2 * b + e
-            spot = ((x + k // 4) % 4) * 4 + (y + k % 4) % 4
-            spots.append(spot)
-
-            @pl.when(k > 0)
-            def _(spot=spot):
-                got(ac.at[spot], ac_rsem.at[spot])
-
-        mats = jnp.concatenate([ac[spots[e], 2 * g] for e in range(2) for g in range(2)], axis=1)
-        both = mm(xfold, mats)
-        queries = jnp.concatenate(
-            [
-                both[0:64, i * 128 : i * 128 + 64] + both[64:128, i * 128 + 64 : i * 128 + 128]
-                for i in range(4)
-            ],
-            axis=0,
-        ).astype(BF16)
-        scores = mm(queries, keys_t[...])
-        top = jnp.max(scores, axis=1, keepdims=True)
-        weights = jnp.exp2(scores - top).astype(BF16)
-        mixed = mm(weights, vals[...])
-        heads = (mixed[:, 0:64] / mixed[:, 64:128]).astype(BF16)
-        for i in range(4):
-            part = heads[i * 64 : i * 64 + 64]
-            folded = jnp.concatenate([part[:, 0:32], part[:, 32:64]], axis=0)
-            acc = acc + mm(folded, ac[spots[i // 2], 2 * (i % 2) + 1])
+        rows0 = slice(g * 512, g * 512 + 512)
+        rows1 = slice(1024 + g * 512, 1024 + g * 512 + 512)
+        vals_t[0:64, rows0] = flipped[0:64]
+        vals_t[0:64, rows1] = flipped[64:128]
+        keys[rows0, :] = block[:, 0:64].astype(BF16)
+        keys[rows1, :] = roll(block, 64)[:, 0:64].astype(BF16)
+    vals_t[64:80, :] = jnp.ones((16, 2048), BF16)
+
+    def spots(b):
+        return [((x + kx) % 4) * 4 + (y + ky) % 4 for kx in ((0, 1) if b % 2 == 0 else (3, 2)) for ky in range(4)]
+
+    def group_of(b):
+        return zhi if b < 2 else 1 - zhi
+
+    def pairs(b, t):
+        slot = 2 * group_of(b) + t
+        here = spots(b)
+        return [(ac[here[i], slot].astype(F32), ac[here[i + 1], slot].astype(F32)) for i in (0, 2, 4, 6)]
+
+    def queries(b):
+        for spot in spots(b)[1 if b % 2 == 0 else 0 :]:
+            got(ac.at[spot, pl.ds(2 * group_of(b), 2)], ac_rsem.at[group_of(b), spot])
+        out = []
+        for f0, f1 in pairs(b, 0):
+            upper_rows = jnp.where(left, f0, roll(f1, 64))
+            lower_rows = jnp.where(left, roll(f0, 64), f1)
+            mats = jnp.concatenate([upper_rows, lower_rows], axis=0).astype(BF16)
+            out.append(mm(mats, xpair).astype(BF16))
+        return jnp.concatenate(out, axis=1)
+
+    def score_chunk(b, q, j, top):
+        rows = slice(j * 256, j * 256 + 256)
+        s = mm(keys[rows, :], q)
+        scores[b % 2, rows, :] = s
+        here = jnp.max(s.reshape(32, 8, 512), axis=0)
+        return here if top is None else jnp.maximum(top, here)
+
+    def value_chunk(b, top, j, total):
+        rows = slice(j * 256, j * 256 + 256)
+        weights = jnp.exp2(scores[b % 2, rows, :] - top).astype(BF16)
+        part = mm(vals_t[:, rows], weights)
+        return part if total is None else total + part
+
+    def finish(b, total, acc):
+        mixed = (total[0:64] / total[64:65]).astype(BF16)
+        for i, (f0, f1) in enumerate(pairs(b, 1)):
+            mats = jnp.concatenate([f0, roll(f0, 64), f1, roll(f1, 64)], axis=0)[:, 0:64].astype(BF16)
+            acc = acc + mm(mats, mixed[:, i * 128 : i * 128 + 128])
         return acc
 
-    acc = lax.fori_loop(0, 8, attend, jnp.zeros((128, 128), F32))
-    total_vel = vel[...] + acc[0:64, 0:64] + acc[64:128, 64:128]
+    acc = jnp.zeros((128, 128), F32)
+    for b in range(4):
+        if b % 2 == 0:
+            q = queries(b)
+            top = None
+            for j in range(8):
+                top = score_chunk(b, q, j, top)
+        peak = jnp.max(top, axis=0, keepdims=True)
+        if b % 2 == 0:
+            q = queries(b + 1)
+        top = None
+        total = None
+        for j in range(8):
+            if b % 2 == 0:
+                top = score_chunk(b + 1, q, j, top)
+            total = value_chunk(b, peak, j, total)
+        acc = finish(b, total, acc)
+    total_vel = vel[...] + (acc[0:64, 0:64] + acc[64:128, 64:128]).T
     vel_fold = jnp.concatenate([total_vel[0:32], total_vel[32:64]], axis=1)
     sca_f = vel_fold
     fin[0:32, :] = sca_f
@@ -350,7 +387,7 @@
     got(vel_r, core_rsem.at[1])
     sign = jnp.where(core == 0, 1.0, -1.0).astype(F32)
     dmd = level * (sign * (vel_fold - vel_r[...]))
-    dmd_out[...] = jnp.where(core == 0, dmd[:, 0:64], dmd[:, 64:128])
+    dmd_full = jnp.where(core == 0, dmd, roll(dmd, 64))
     sca[me_p] = (dmd * LOSS_SCALE).astype(BF16)
     sca_ref = sca.at[me_p]
     to_plane(sca_ref, sca_ref, sca_ssem, sca_rsem)
@@ -373,6 +410,9 @@
     gpart[0:128, :] = grads[:, 0:128].astype(BF16)
     gpart[128:160, :] = rest.astype(BF16)
 
+    sent(fin.at[0:32], core_ssem.at[1])
+    fin[0:32, :] = dmd_full
+
     zme = zhi * 4 + zlo
     for k in range(4):
 
@@ -401,14 +441,6 @@
     def _():
         got(fin.at[32:192], core_rsem.at[2])
 
-    gin_out[:, 0:128] = fin[32:96, :]
-    gout_out[:, 0:128] = fin[96:160, :]
-    tail = fin[160:192, :]
-    for i in range(4):
-        ref = gin_out if i < 2 else gout_out
-        piece = tail if i == 0 else roll(tail, 128 - 32 * i)
-        ref[(i % 2) * 32 : (i % 2) * 32 + 32, 128:160] = piece[:, 0:32]
-
     for m in range(2):
         for t in range(2):
 
@@ -431,12 +463,22 @@
         sent(fin.at[32:192], core_ssem.at[2])
 
     sent(msg, core_ssem.at[0])
-    sent(fin.at[0:32], core_ssem.at[1])
     sent(own_ref, tokz_ssem)
     sent(tok.at[0:2, 0:15], tok_ssem)
     sent(ac.at[0:15], ac_ssem)
     sent(noi.at[0:15], noi_ssem)
     sent(sca.at[0:15], sca_ssem)
+
+
+def unpack(packed, dmd_out, gin_out, gout_out):
+    dmd_out[...] = packed[0:32, 0:64]
+    gin_out[:, 0:128] = packed[32:96, :]
+    gout_out[:, 0:128] = packed[96:160, :]
+    tail = packed[160:192, :]
+    for i in range(4):
+        ref = gin_out if i < 2 else gout_out
+        piece = tail if i == 0 else roll(tail, 128 - 32 * i)
+        ref[(i % 2) * 32 : (i % 2) * 32 + 32, 128:160] = piece[:, 0:32]
 
 
 def body(
@@ -458,18 +500,17 @@
         return qkv.transpose(1, 2, 0, 3).reshape(3, 640, 128)
 
     vmem = pl.BlockSpec(memory_space=pltpu.VMEM)
-    hbm = pl.BlockSpec(memory_space=pl.ANY)
+    hbm = pl.BlockSpec(memory_space=pltpu.HBM)
     dma = pltpu.SemaphoreType.DMA
-    dmd, grad_in, grad_out = pl.pallas_call(
+    packed = pl.pallas_call(
         kernel,
-        out_shape=(
-            jax.ShapeDtypeStruct((32, 64), F32),
-            jax.ShapeDtypeStruct((64, 160), F32),
-            jax.ShapeDtypeStruct((64, 160), F32),
-        ),
-        in_specs=[pl.BlockSpec(memory_space=pltpu.SMEM), vmem, vmem] + [hbm] * 10,
-        out_specs=(vmem, vmem, vmem),
+        out_shape=jax.ShapeDtypeStruct((192, 128), F32),
+        in_specs=[hbm] * 13,
+        out_specs=vmem,
         scratch_shapes=[
+            pltpu.SMEM((4,), jnp.int32),
+            pltpu.VMEM((32, 64), BF16),
+            pltpu.VMEM((32, 64), BF16),
             pltpu.VMEM((64, 5120), BF16),
             pltpu.VMEM((64, 5120), BF16),
             pltpu.VMEM((64, 5120), BF16),
@@ -485,8 +526,9 @@
             pltpu.VMEM((32, 128), BF16),
             pltpu.VMEM((2, 16, 32, 128), BF16),
             pltpu.VMEM((16, 32, 128), BF16),
-            pltpu.VMEM((64, 2048), BF16),
-            pltpu.VMEM((2048, 128), BF16),
+            pltpu.VMEM((2048, 64), BF16),
+            pltpu.VMEM((80, 2048), BF16),
+            pltpu.VMEM((2, 2048, 512), F32),
             pltpu.VMEM((2, 512, 256), BF16),
             pltpu.VMEM((2, 512, 256), F32),
             pltpu.VMEM((64, 64), F32),
@@ -494,14 +536,13 @@
             pltpu.VMEM((16, 32, 128), BF16),
             pltpu.VMEM((160, 128), BF16),
             pltpu.VMEM((8, 160, 128), BF16),
-            pltpu.VMEM((192, 128), F32),
-            dma((12,)),
+            dma((15,)),
             dma((4,)),
             dma((8,)),
             dma,
             dma((4,)),
             dma,
-            dma((16,)),
+            dma((2, 16)),
             dma((3,)),
             dma((3,)),
             dma,
@@ -519,20 +560,35 @@
             collective_id=0, has_side_effects=True, vmem_limit_bytes=48 * 1024 * 1024
         ),
     )(
-        steps_t,
-        noise_gen[0],
-        noise_add[0],
-        gen_in,
-        gen_out.T,
-        real_in,
-        table(real_qkv),
-        real_proj[0],
-        real_head.T,
-        fake_in,
-        table(fake_qkv),
-        fake_proj[0],
-        fake_head.T,
+        *(
+            pltpu.with_memory_space_constraint(operand, pltpu.HBM)
+            for operand in (
+                steps_t,
+                noise_gen[0],
+                noise_add[0],
+                gen_in,
+                gen_out.T,
+                real_in,
+                table(real_qkv),
+                real_proj[0],
+                real_head.T,
+                fake_in,
+                table(fake_qkv),
+                fake_proj[0],
+                fake_head.T,
+            )
+        )
     )
+    dmd, grad_in, grad_out = pl.pallas_call(
+        unpack,
+        out_shape=(
+            jax.ShapeDtypeStruct((32, 64), F32),
+            jax.ShapeDtypeStruct((64, 160), F32),
+            jax.ShapeDtypeStruct((64, 160), F32),
+        ),
+        in_specs=[vmem],
+        out_specs=(vmem, vmem, vmem),
+    )(pltpu.with_memory_space_constraint(packed, pltpu.VMEM))
     return dmd[None], grad_in, grad_out.T
 
 

time: 69.1 us -> 48.3 us (0.70)
  local copies, waits for them, and re-layouts: 13 us -> 0 us
  Pallas kernels: 54.9 us -> 47.6 us
    unnamed x29 -> x0, local copies, waits for them, and re-layouts: 13 us -> none
    pallas_call x1 -> x2, Pallas kernels: 54.9 us -> 47.6 us  [the longest x1 46.9 us: body(): pl.pallas_call(kernel, out_shape=jax.ShapeDtypeStruct((192, 128), F32), i...]
where the time goes in v2:
time: 48.3 us; the launch traced here: 48.2 us
  Pallas kernels  47.6 us (99%)
  between operations  0.64 us (1%)
    pallas_call x1, Pallas kernels, body(): pl.pallas_call(kernel, out_shape=jax.ShapeDtypeStruct((192, 128), F32), i...  46.9 us

profile of v2, /device:TPU:1, one launch (start us, length us, event | category | flops | bytes accessed | tf_op | source)
XLA Modules:
  0.0 48.2 jit_solution(7317538718767041548)
XLA Ops:
  0.6 46.9 %shard_map.148.packed = f32[192,128]{1,0:T(8,128)S(1)} custom-call(s32[4]{0:T(128)} %steps.1, bf16[32,64]{1,0:T(8,128)(2,1)} %bitcast.26, bf16[32,64]{1,0:T(8,128)(2,1)} %bitcast.27, bf16[64,5120]{1,0:T(8,128)(2,1)} %gen_in.1, bf16[64,5120]{1,0:T(8,128)(2,1)} %bitcast.19, bf16[64,5120]{1,0:T(8,128)(2,1)} %real_in.1, bf16[3,640,128]{2,1,0:T(8,128)(2,1)} %bitcast.22, ...), custom_call_target="tpu_custom_call" | custom-call | tf_op jit(solution)/shard_map/pallas_call | solution.py:505
  47.5 0.7 %shard_map.149 = (f32[32,64]{1,0:T(8,128)}, f32[64,160]{1,0:T(8,128)}, f32[64,160]{1,0:T(8,128)}) custom-call(f32[192,128]{1,0:T(8,128)S(1)} %shard_map.148.packed), custom_call_target="tpu_custom_call" | custom-call | tf_op jit(solution)/shard_map/pallas_call | solution.py:582

commit v3 on v2

--- a/solution.py
+++ b/solution.py
@@ -99,18 +99,22 @@
 ):
     mp = lax.axis_index("mp")
     seq = lax.axis_index("seq")
-    core = mp % 2
-    zlo = mp // 2
-    x = seq // 8
-    zhi = (seq // 4) % 2
-    y = seq % 4
+    core = mp & 1
+    zlo = mp >> 1
+    x = seq >> 3
+    zhi = (seq >> 2) & 1
+    y = seq & 3
     me_p = x * 4 + y
 
     def dev(x_, y_, zhi_, zlo_, core_):
         return (zlo_ * 2 + core_, x_ * 8 + zhi_ * 4 + y_)
 
+    def gray(v):
+        return v ^ (v >> 1)
+
     def plane_dev(k):
-        return dev((x + k // 4) % 4, (y + k % 4) % 4, zhi, zlo, core)
+        near = 15 - k
+        return dev((x + gray(near >> 2)) & 3, (y + gray(near & 3)) & 3, zhi, zlo, core)
 
     partner = dev(x, y, zhi, zlo, 1 - core)
     across = dev(x, y, 1 - zhi, zlo, core)
@@ -125,7 +129,7 @@
             rc(src, dst, ssem, rsem, plane_dev(k)).start()
             return carry
 
-        lax.fori_loop(1, 16, send, 0)
+        lax.fori_loop(0, 15, send, 0, unroll=True)
 
     def got(ref, rsem):
         rc(ref, ref, rsem, rsem, partner).wait_recv()
@@ -172,16 +176,16 @@
         return carry
 
     def greet_mp(k, carry):
-        greet(((mp + k) % 8, seq))
+        greet(((mp + k) & 7, seq))
         return carry
 
     def greet_across(k, carry):
         greet(dev(x, y, 1 - zhi, k, core))
         return carry
 
-    lax.fori_loop(0, 4, greet_across, 0)
-    lax.fori_loop(1, 16, greet_plane, 0)
-    lax.fori_loop(1, 8, greet_mp, 0)
+    lax.fori_loop(0, 4, greet_across, 0, unroll=True)
+    lax.fori_loop(0, 15, greet_plane, 0, unroll=True)
+    lax.fori_loop(1, 8, greet_mp, 0, unroll=True)
 
     for m in range(2):
         for k in range(4):
@@ -268,11 +272,11 @@
         piece = ac.at[me_p, slot_here]
 
         def spread(k, carry):
-            z = (zhi * 4 + zlo + k) % 8
-            rc(piece, piece, z_ssem, z_rsem.at[slot_here], dev(x, y, z // 4, z % 4, core)).start()
+            z = (zhi * 4 + zlo + k) & 7
+            rc(piece, piece, z_ssem, z_rsem.at[slot_here], dev(x, y, z >> 2, z & 3, core)).start()
             return carry
 
-        lax.fori_loop(1, 8, spread, 0)
+        lax.fori_loop(1, 8, spread, 0, unroll=True)
 
     far_ref = tok.at[1 - zhi, me_p]
     got(far_ref, tokz_rsem)
@@ -303,8 +307,11 @@
         keys[rows1, :] = roll(block, 64)[:, 0:64].astype(BF16)
     vals_t[64:80, :] = jnp.ones((16, 2048), BF16)
 
+    near = ((0, 0), (0, 1), (0, 3), (1, 0), (3, 0), (0, 2), (1, 1), (3, 3))
+    far = ((1, 3), (3, 1), (2, 0), (1, 2), (3, 2), (2, 1), (2, 3), (2, 2))
+
     def spots(b):
-        return [((x + kx) % 4) * 4 + (y + ky) % 4 for kx in ((0, 1) if b % 2 == 0 else (3, 2)) for ky in range(4)]
+        return [((x + kx) & 3) * 4 + ((y + ky) & 3) for kx, ky in (near if b % 2 == 0 else far)]
 
     def group_of(b):
         return zhi if b < 2 else 1 - zhi
@@ -347,18 +354,18 @@
 
     acc = jnp.zeros((128, 128), F32)
     for b in range(4):
-        if b % 2 == 0:
+        if b in (0,):
             q = queries(b)
             top = None
             for j in range(8):
                 top = score_chunk(b, q, j, top)
         peak = jnp.max(top, axis=0, keepdims=True)
-        if b % 2 == 0:
+        if b in (0, 1, 2):
             q = queries(b + 1)
         top = None
         total = None
         for j in range(8):
-            if b % 2 == 0:
+            if b in (0, 1, 2):
                 top = score_chunk(b + 1, q, j, top)
             total = value_chunk(b, peak, j, total)
         acc = finish(b, total, acc)

time: 48.3 us -> 46.4 us (0.961)
  Pallas kernels: 47.6 us -> 45.7 us
    pallas_call x1, Pallas kernels: 46.9 us -> 45 us  [body(): pl.pallas_call(kernel, out_shape=jax.ShapeDtypeStruct((192, 128), F32), i...]
where the time goes in v3:
time: 46.4 us; the launch traced here: 46.3 us
  Pallas kernels  45.7 us (98%)
  between operations  0.64 us (1%)
    pallas_call x1, Pallas kernels, body(): pl.pallas_call(kernel, out_shape=jax.ShapeDtypeStruct((192, 128), F32), i...  45 us

profile of v3, /device:TPU:1, one launch (start us, length us, event | category | flops | bytes accessed | tf_op | source)
XLA Modules:
  0.0 46.3 jit_solution(11988859881340082620)
XLA Ops:
  0.6 45.0 %shard_map.148.packed = f32[192,128]{1,0:T(8,128)S(1)} custom-call(s32[4]{0:T(128)} %steps.1, bf16[32,64]{1,0:T(8,128)(2,1)} %bitcast.26, bf16[32,64]{1,0:T(8,128)(2,1)} %bitcast.27, bf16[64,5120]{1,0:T(8,128)(2,1)} %gen_in.1, bf16[64,5120]{1,0:T(8,128)(2,1)} %bitcast.19, bf16[64,5120]{1,0:T(8,128)(2,1)} %real_in.1, bf16[3,640,128]{2,1,0:T(8,128)(2,1)} %bitcast.22, ...), custom_call_target="tpu_custom_call" | custom-call | tf_op jit(solution)/shard_map/pallas_call | solution.py:512
  45.6 0.7 %shard_map.149 = (f32[32,64]{1,0:T(8,128)}, f32[64,160]{1,0:T(8,128)}, f32[64,160]{1,0:T(8,128)}) custom-call(f32[192,128]{1,0:T(8,128)S(1)} %shard_map.148.packed), custom_call_target="tpu_custom_call" | custom-call | tf_op jit(solution)/shard_map/pallas_call | solution.py:589

commit v4 on v3

--- a/solution.py
+++ b/solution.py
@@ -402,46 +402,54 @@
 
     scaled_rows = sca[...].reshape(512, 128)
     scaled_t = scaled_rows.astype(F32).T.astype(BF16)
+    zme = zhi * 4 + zlo
+
+    def to_owners(part, grads):
+        lane32 = lanes((16, 128))
+        rest = grads[0:16, 128:256]
+        for i in range(1, 4):
+            rest = jnp.where(lane32 < 32 * i, rest, roll(grads[16 * i : 16 * i + 16, 128:256], 32 * i))
+        gpart[part, 0:64, :] = grads[:, 0:128].astype(BF16)
+        gpart[part, 64:80, :] = rest.astype(BF16)
+        for k in range(4):
+
+            @pl.when(jnp.logical_not((zhi == core) & (zlo == k)))
+            def _(k=k):
+                rc(
+                    gpart.at[part],
+                    grecv.at[zme, part],
+                    g_ssem.at[part, k],
+                    g_rsem.at[part, zme],
+                    dev(x, y, core, k, core),
+                ).start()
+
+    grad_out = mm(scaled_t[0:64], hid[0]) + mm(scaled_t[64:128], hid[1])
+    to_owners(1, grad_out)
     grad_in = jnp.zeros((64, 256), F32)
-    grad_out = jnp.zeros((64, 256), F32)
     for h in range(2):
-        grad_out = grad_out + mm(scaled_t[h * 64 : h * 64 + 64], hid[h])
         weight = jnp.concatenate([gout_s, zeros] if h == 0 else [zeros, gout_s], axis=0)
         pre = (mm(scaled_rows, weight) * dsil[h]).astype(BF16)
         grad_in = grad_in + mm(noise_t[h * 64 : h * 64 + 64], pre)
-    grads = jnp.concatenate([grad_in, grad_out], axis=0)
-    lane32 = lanes((32, 128))
-    rest = grads[0:32, 128:256]
-    for i in range(1, 4):
-        rest = jnp.where(lane32 < 32 * i, rest, roll(grads[32 * i : 32 * i + 32, 128:256], 32 * i))
-    gpart[0:128, :] = grads[:, 0:128].astype(BF16)
-    gpart[128:160, :] = rest.astype(BF16)
-
+    to_owners(0, grad_in)
     sent(fin.at[0:32], core_ssem.at[1])
     fin[0:32, :] = dmd_full
 
-    zme = zhi * 4 + zlo
-    for k in range(4):
-
-        @pl.when(jnp.logical_not((zhi == core) & (zlo == k)))
-        def _(k=k):
-            rc(gpart, grecv.at[zme], g_ssem.at[k], g_rsem.at[zme], dev(x, y, core, k, core)).start()
-
     @pl.when(zhi == core)
     def _():
-        total = gpart[...].astype(F32)
-        for src in range(8):
-
-            @pl.when(src != zme)
-            def _(src=src):
-                got(grecv.at[src], g_rsem.at[src])
-
-            @pl.when(src == zme)
-            def _(src=src):
-                grecv[src] = jnp.zeros((160, 128), BF16)
-
-            total = total + grecv[src].astype(F32)
-        fin[32:192, :] = total
+        for part in (1, 0):
+            total = gpart[part].astype(F32)
+            for src in range(8):
+
+                @pl.when(src != zme)
+                def _(src=src, part=part):
+                    got(grecv.at[src, part], g_rsem.at[part, src])
+
+                @pl.when(src == zme)
+                def _(src=src, part=part):
+                    grecv[src, part] = jnp.zeros((80, 128), BF16)
+
+                total = total + grecv[src, part].astype(F32)
+            fin[32 + 80 * part : 112 + 80 * part, :] = total
         rc(fin.at[32:192], fin.at[32:192], core_ssem.at[2], core_rsem.at[2], partner).start()
 
     @pl.when(zhi != core)
@@ -463,7 +471,8 @@
 
         @pl.when(jnp.logical_not((zhi == core) & (zlo == k)))
         def _(k=k):
-            sent(gpart, g_ssem.at[k])
+            sent(gpart.at[0], g_ssem.at[0, k])
+            sent(gpart.at[1], g_ssem.at[1, k])
 
     @pl.when(zhi == core)
     def _():
@@ -479,13 +488,12 @@
 
 def unpack(packed, dmd_out, gin_out, gout_out):
     dmd_out[...] = packed[0:32, 0:64]
-    gin_out[:, 0:128] = packed[32:96, :]
-    gout_out[:, 0:128] = packed[96:160, :]
-    tail = packed[160:192, :]
-    for i in range(4):
-        ref = gin_out if i < 2 else gout_out
-        piece = tail if i == 0 else roll(tail, 128 - 32 * i)
-        ref[(i % 2) * 32 : (i % 2) * 32 + 32, 128:160] = piece[:, 0:32]
+    for ref, at in ((gin_out, 32), (gout_out, 112)):
+        ref[:, 0:128] = packed[at : at + 64, :]
+        tail = packed[at + 64 : at + 80, :]
+        for i in range(4):
+            piece = tail if i == 0 else roll(tail, 128 - 32 * i)
+            ref[16 * i : 16 * i + 16, 128:160] = piece[:, 0:32]
 
 
 def body(
@@ -541,8 +549,8 @@
             pltpu.VMEM((64, 64), F32),
             pltpu.VMEM((32, 128), F32),
             pltpu.VMEM((16, 32, 128), BF16),
-            pltpu.VMEM((160, 128), BF16),
-            pltpu.VMEM((8, 160, 128), BF16),
+            pltpu.VMEM((2, 80, 128), BF16),
+            pltpu.VMEM((8, 2, 80, 128), BF16),
             dma((15,)),
             dma((4,)),
             dma((8,)),
@@ -560,8 +568,8 @@
             dma,
             dma,
             dma,
-            dma((4,)),
-            dma((8,)),
+            dma((2, 4)),
+            dma((2, 8)),
         ],
         compiler_params=pltpu.CompilerParams(
             collective_id=0, has_side_effects=True, vmem_limit_bytes=48 * 1024 * 1024

time: 46.4 us -> 46.8 us (level)
  no operation moved by 1% of the time
where the time goes in v4:
time: 46.8 us; the launch traced here: 46.7 us
  Pallas kernels  46 us (98%)
  between operations  0.64 us (1%)
    pallas_call x1, Pallas kernels, body(): pl.pallas_call(kernel, out_shape=jax.ShapeDtypeStruct((192, 128), F32), i...  45.3 us

profile of v4, /device:TPU:1, one launch (start us, length us, event | category | flops | bytes accessed | tf_op | source)
XLA Modules:
  0.0 46.7 jit_solution(4759687506926310709)
XLA Ops:
  0.6 45.3 %shard_map.148.packed = f32[192,128]{1,0:T(8,128)S(1)} custom-call(s32[4]{0:T(128)} %steps.1, bf16[32,64]{1,0:T(8,128)(2,1)} %bitcast.26, bf16[32,64]{1,0:T(8,128)(2,1)} %bitcast.27, bf16[64,5120]{1,0:T(8,128)(2,1)} %gen_in.1, bf16[64,5120]{1,0:T(8,128)(2,1)} %bitcast.19, bf16[64,5120]{1,0:T(8,128)(2,1)} %real_in.1, bf16[3,640,128]{2,1,0:T(8,128)(2,1)} %bitcast.22, ...), custom_call_target="tpu_custom_call" | custom-call | tf_op jit(solution)/shard_map/pallas_call | solution.py:520
  45.9 0.7 %shard_map.149 = (f32[32,64]{1,0:T(8,128)}, f32[64,160]{1,0:T(8,128)}, f32[64,160]{1,0:T(8,128)}) custom-call(f32[192,128]{1,0:T(8,128)S(1)} %shard_map.148.packed), custom_call_target="tpu_custom_call" | custom-call | tf_op jit(solution)/shard_map/pallas_call | solution.py:597

commit v5 on v3

--- a/solution.py
+++ b/solution.py
@@ -207,6 +207,7 @@
     noised = (1.0 - level) * clean + level * nadd_v[...].astype(F32)
     msg[...] = jnp.concatenate([noised, own_noise.astype(F32)], axis=1).astype(BF16)
 
+    scores[...] = jnp.zeros((2, 2048, 512), F32)
     pl.semaphore_wait(barrier, 26)
 
     for m in range(2):

time: 46.4 us -> 46 us (level)
  no operation moved by 1% of the time
where the time goes in v5:
time: 46 us; the launch traced here: 45.9 us
  Pallas kernels  45.3 us (98%)
  between operations  0.64 us (1%)
    pallas_call x1, Pallas kernels, body(): pl.pallas_call(kernel, out_shape=jax.ShapeDtypeStruct((192, 128), F32), i...  44.5 us

profile of v5, /device:TPU:1, one launch (start us, length us, event | category | flops | bytes accessed | tf_op | source)
XLA Modules:
  0.0 45.9 jit_solution(3986006489863040292)
XLA Ops:
  0.6 44.5 %shard_map.148.packed = f32[192,128]{1,0:T(8,128)S(1)} custom-call(s32[4]{0:T(128)} %steps.1, bf16[32,64]{1,0:T(8,128)(2,1)} %bitcast.26, bf16[32,64]{1,0:T(8,128)(2,1)} %bitcast.27, bf16[64,5120]{1,0:T(8,128)(2,1)} %gen_in.1, bf16[64,5120]{1,0:T(8,128)(2,1)} %bitcast.19, bf16[64,5120]{1,0:T(8,128)(2,1)} %real_in.1, bf16[3,640,128]{2,1,0:T(8,128)(2,1)} %bitcast.22, ...), custom_call_target="tpu_custom_call" | custom-call | tf_op jit(solution)/shard_map/pallas_call | solution.py:513
  45.2 0.7 %shard_map.149 = (f32[32,64]{1,0:T(8,128)}, f32[64,160]{1,0:T(8,128)}, f32[64,160]{1,0:T(8,128)}) custom-call(f32[192,128]{1,0:T(8,128)S(1)} %shard_map.148.packed), custom_call_target="tpu_custom_call" | custom-call | tf_op jit(solution)/shard_map/pallas_call | solution.py:590
